TPU v7x, 32 devices: a whole 2x2x4 slice. The times are simulated.
32 devices in a mesh: groups: 2 (over x), row: 16 (over z, y, core).
Axes of the slice: x: 2, y: 2, z: 4, core: 2. Of those that a mesh axis runs over, the one named last changes fastest.
Arguments:
- homolog_embedding: bfloat16 [512, 128, 64], P('groups', 'row'), parts along dimension 0, may hold values from -6 to 6
- coupling_embedding: bfloat16 [256, 128, 128], P(('groups', 'row')), parts along dimension 0, may hold values from -4.2 to 4.2
- entry_indicator: int32 [512, 128], P('groups', 'row'), parts along dimension 0, may hold values 0 or 1
- nonpadding_indicator: int32 [256], P(('groups', 'row')), parts along dimension 0, may hold values 0 or 1
- first_factor_matrix: bfloat16 [64, 32], replicated, may hold values from -0.75 to 0.75
- second_factor_matrix: bfloat16 [64, 32], replicated, may hold values from -0.75 to 0.75
- tensor_product_matrix: bfloat16 [1024, 128], replicated, may hold values from -1.5 to 1.5
- coupling_to_groups: bfloat16 [128, 8], replicated, may hold values from -15 to 15
- query_key_gate_matrix: bfloat16 [64, 1024], replicated, may hold values from -0.75 to 0.75
- attention_final_matrix: bfloat16 [256, 64], replicated, may hold values from -0.375 to 0.375
Outputs:
- pair_output: bfloat16 [256, 128, 128], P(('groups', 'row')), parts along dimension 0
- refreshed_homologs: bfloat16 [512, 128, 64], P('groups', 'row'), parts along dimension 0
There are 2 independent parts, one for each index of `groups`. A program takes and returns all parts, laid end to end along the dimension named above; an argument that names none is the same for every part. Nothing has to cross between parts.
All inputs are finite; a program needn't handle non-finite values. No bound on the sum of `entry_indicator` or of `nonpadding_indicator` on one device may be relied on, other than what follows from the above.
Results may differ from a plain program's by a relative error of at most 0.019.
The roundings to bfloat16 on the way count: a program that leaves them out, or rounds other values in their place, can miss the bound.
Values may be sent and summed in bfloat16 or wider, within the bound.
A program may use at most 128 MiB of HBM per device.

v0:
```python
import math

import jax
import jax.numpy as jnp
from jax import lax
from jax.sharding import PartitionSpec as P

ATTN_GROUPS = 8
ATTN_DIM = 32


epsilon = 1e-05


def standardize_features(values):
    widened = values.astype(jnp.float32)
    average = jnp.mean(widened, axis=-1, keepdims=True)
    centred = widened - average
    spread = jnp.mean(centred * centred, axis=-1, keepdims=True)
    return centred * lax.rsqrt(spread + epsilon)


def opm_tile(left_rows, left_mask, right_piece, mask_portion, tensor_product_matrix):
    seq_count = right_piece.shape[0]
    column_count = right_piece.shape[1]
    factor_width = right_piece.shape[2]
    flat_right = right_piece.reshape(seq_count, column_count * factor_width)

    def one_row(row_index):
        left_row = lax.dynamic_index_in_dim(left_rows, row_index, 1, keepdims=False)
        mask_row = lax.dynamic_index_in_dim(left_mask, row_index, 1, keepdims=False)
        outer_prod = jnp.dot(left_row.T, flat_right, preferred_element_type=jnp.float32)
        outer_prod = jnp.transpose(
            outer_prod.reshape(factor_width, column_count, factor_width), (1, 0, 2)
        )
        pair_count = jnp.dot(mask_row, mask_portion, preferred_element_type=jnp.float32)
        averaged = (outer_prod / jnp.maximum(pair_count, 1.0)[:, None, None]).astype(jnp.bfloat16)
        averaged = averaged.reshape(column_count, factor_width * factor_width)
        return jnp.dot(averaged, tensor_product_matrix, preferred_element_type=jnp.float32)

    return lax.map(one_row, jnp.arange(left_rows.shape[1], dtype=jnp.int32))


def on_device(
    homolog_embedding,
    coupling_embedding,
    entry_indicator,
    nonpadding_indicator,
    first_factor_matrix,
    second_factor_matrix,
    tensor_product_matrix,
    coupling_to_groups,
    query_key_gate_matrix,
    attention_final_matrix,
):
    standardized_homologs = standardize_features(homolog_embedding).astype(jnp.bfloat16)
    active_float = (entry_indicator * nonpadding_indicator[None, :]).astype(jnp.float32)
    active_bfloat = active_float.astype(jnp.bfloat16)
    left_operand = (
        jnp.dot(standardized_homologs, first_factor_matrix, preferred_element_type=jnp.float32)
        * active_float[..., None]
    ).astype(jnp.bfloat16)
    normalized_portion, mask_portion = lax.all_gather(
        (standardized_homologs, active_bfloat), "row", axis=1, tiled=True
    )
    right_piece = (
        jnp.dot(normalized_portion, second_factor_matrix, preferred_element_type=jnp.float32)
        * mask_portion.astype(jnp.float32)[..., None]
    ).astype(jnp.bfloat16)
    update = opm_tile(left_operand, active_bfloat, right_piece, mask_portion, tensor_product_matrix)
    pair_output = (coupling_embedding.astype(jnp.float32) + update).astype(jnp.bfloat16)
    normed_pair = standardize_features(pair_output).astype(jnp.bfloat16)
    bias_local = jnp.einsum(
        "ijc,ch->hij", normed_pair, coupling_to_groups, preferred_element_type=jnp.float32
    ).astype(jnp.bfloat16)
    shifted_alignment, shifted_mask = (
        lax.all_to_all(standardized_homologs, "row", split_axis=0, concat_axis=1, tiled=True),
        lax.all_to_all(active_bfloat, "row", split_axis=0, concat_axis=1, tiled=True),
    )
    projected_values = jnp.dot(
        shifted_alignment, query_key_gate_matrix, preferred_element_type=jnp.float32
    ).astype(jnp.bfloat16)
    bias_full = lax.all_gather(bias_local, "row", axis=1, tiled=True)
    residues = projected_values.shape[1]
    scale = 1.0 / math.sqrt(ATTN_DIM)
    half_heads = ATTN_GROUPS // 2

    def attend(sequence):
        projected_row, key_mask = sequence
        blocks = projected_row.reshape(residues, 4, ATTN_GROUPS, ATTN_DIM)
        outputs = []
        for group_index in range(2):
            head_start = group_index * half_heads
            queries = blocks[:, 0, head_start : head_start + half_heads]
            keys_part = blocks[:, 1, head_start : head_start + half_heads]
            values_part = blocks[:, 2, head_start : head_start + half_heads]
            gates_part = blocks[:, 3, head_start : head_start + half_heads]
            logits = (
                jnp.einsum("ihd,jhd->hij", queries, keys_part, preferred_element_type=jnp.float32)
                * scale
            )
            logits = logits + bias_full[head_start : head_start + half_heads].astype(jnp.float32)
            logits = jnp.where(key_mask[None, None, :] > 0, logits, -1000000000.0)
            weights = jax.nn.softmax(logits, axis=-1).astype(jnp.bfloat16)
            attended = jnp.einsum(
                "hij,jhd->ihd", weights, values_part, preferred_element_type=jnp.float32
            )
            outputs.append(attended * jax.nn.sigmoid(gates_part.astype(jnp.float32)))
        gated = jnp.concatenate(outputs, axis=1).astype(jnp.bfloat16)
        return gated.reshape(residues, ATTN_GROUPS * ATTN_DIM)

    gated_out = lax.map(attend, (projected_values, shifted_mask))
    returned = lax.all_to_all(gated_out, "row", split_axis=1, concat_axis=0, tiled=True)
    increment_term = jnp.dot(returned, attention_final_matrix, preferred_element_type=jnp.float32)
    refreshed_homologs = (homolog_embedding.astype(jnp.float32) + increment_term).astype(
        jnp.bfloat16
    )
    return (pair_output, refreshed_homologs)


def solution(mesh):
    return jax.shard_map(
        on_device,
        mesh=mesh,
        in_specs=(
            P("groups", "row", None),
            P(("groups", "row"), None, None),
            P("groups", "row"),
            P(("groups", "row")),
            P(),
            P(),
            P(),
            P(),
            P(),
            P(),
        ),
        out_specs=(P(("groups", "row"), None, None), P("groups", "row", None)),
        check_vma=False,
    )
```

profile of v0, /device:TPU:1, one launch (start us, length us, event | category | flops | bytes accessed | tf_op | source)
XLA Modules:
  0.0 274.0 jit_solution(6603387715939211449)
XLA Ops:
  7.3 1.3 copy.47
  9.6 1.4 fusion.43
  11.9 7.3 %all-to-all-start.1 = ((bf16[16,16,8]{1,2,0:T(8,128)(2,1)}), bf16[16,16,8]{1,2,0:T(8,128)(2,1)S(1)}, u32[]{:S(2)}, u32[]{:S(2)}) async-start(bf16[16,16,8]{1,2,0:T(8,128)(2,1)} %copy.54), calls=%async_computation.1 | async-start | bytes 65536 | tf_op jit(solution)/shard_map/all_to_all | solution.py:78
  19.2 2.1 reshape.98
  21.4 3.8 %all-to-all-done.1 = bf16[16,16,8]{1,2,0:T(8,128)(2,1)S(1)} async-done(((bf16[16,16,8]{1,2,0:T(8,128)(2,1)}), bf16[16,16,8]{1,2,0:T(8,128)(2,1)S(1)}, u32[]{:S(2)}, u32[]{:S(2)}) %all-to-all-start.1) | async-done | bytes 4128 | tf_op jit(solution)/shard_map/all_to_all | solution.py:78
  25.1 4.2 %all-to-all-start = ((bf16[16,2,4096]{2,1,0:T(2,128)(2,1)}), bf16[16,2,4096]{2,1,0:T(2,128)(2,1)S(1)}, u32[]{:S(2)}, u32[]{:S(2)}) async-start(bf16[16,2,4096]{2,1,0:T(2,128)(2,1)} %reshape.98), calls=%async_computation | async-start | bytes 524288 | tf_op jit(solution)/shard_map/all_to_all | solution.py:77
  29.4 24.8 %all_gather.10 = bf16[256,128]{0,1:T(8,128)(2,1)S(1)} all-gather(bf16[256,8]{0,1:T(8,128)(2,1)S(1)} %get-tuple-element.217), channel_id=1, replica_groups=mesh['groups'=2,'row'=16] {'row'}, dimensions={1}, use_global_device_ids=true | all-gather | bytes 69632 | tf_op jit(solution)/shard_map/all_gather | solution.py:63
  54.4 1.3 fusion.40
  56.2 3.2 %convolution_convert_fusion = bf16[16,128,1024]{2,1,0:T(8,128)(2,1)} fusion(bf16[16,16,8,64]{3,2,1,0:T(8,128)(2,1)S(1)} %bitcast.181, bf16[64,1024]{1,0:T(8,128)(2,1)S(1)} %copy-done), kind=kOutput, calls=%fused_computation.52 | convolution fusion | flops 270532608 | bytes 4587520 | tf_op jit(solution)/shard_map/dot_general | solution.py:80
  59.4 40.1 %all-gather.2.cloned.1.call-done = bf16[256,128,64]{2,1,0:T(8,128)(2,1)} async-done(((bf16[256,8,64]{2,1,0:T(8,128)(2,1)}), bf16[256,128,64]{2,1,0:T(8,128)(2,1)}) %all-gather.2.cloned.1.call-update) | async-done | bytes 4194320 | tf_op jit(solution)/shard_map/all_gather | solution.py:63
  99.6 6.4 %multiply_convert_fusion = bf16[256,128,32]{1,2,0:T(8,128)(2,1)S(1)} fusion(bf16[256,128,64]{2,1,0:T(8,128)(2,1)} %all-gather.2.cloned.1.call-done, f32[256,128]{1,0:T(8,128)S(1)} %copy.49, bf16[64,32]{0,1:T(8,128)(2,1)S(1)} %copy-done.7), kind=kOutput, calls=%fused_computation.51 | convolution fusion | flops 136314880 | bytes 6426624 | tf_op jit(solution)/shard_map/dot_general | solution.py:67
  106.0 3.6 %copy.50 = bf16[256,128,32]{0,2,1:T(8,128)(2,1)} copy(bf16[256,128,32]{1,2,0:T(8,128)(2,1)S(1)} %multiply_convert_fusion) | data formatting | bytes 4194304 | tf_op jit(solution)/shard_map/convert_element_type | solution.py:69
  109.6 61.1 %while.20 = (s32[]{:T(128)}, f32[8,128,128]{2,1,0:T(8,128)}, s32[8]{0:T(128)S(1)}, bf16[256,8,32]{0,2,1:T(8,128)(2,1)S(1)}, bf16[256,4096]{0,1:T(8,128)(2,1)}, /...) while((s32[]{:T(128)}, f32[8,128,128]{2,1,0:T(8,128)}, ...), condition=%wide.region_3.4_spmd, body=%wide.region_2.3_spmd.sunk | while | flops 100991104 | bytes 3558051 | solution.py:41
  112.3 4.0 %fusion.95 = bf16[128,32,32]{0,1,2:T(8,128)(2,1)S(1)} fusion(bf16[128,32,256]{2,1,0:T(8,128)(2,1)} %bitcast.183, f32[128]{0:T(128)S(1)} %fusion.94, bf16[256,8,32]{0,2,1:T(8,128)(2,1)S(1)} %get-tuple-element.237, s32[]{:T(128)S(6)} %select_n.28), kind=kOutput, calls=%fused_computation.4.clone.1 | convolution fusion | flops 67371008 | bytes 2376196 | tf_op jit(solution)/shard_map/while/body/eval_jaxpr/dot_general | solution.py:32
  119.9 4.0 %fusion.95 = bf16[128,32,32]{0,1,2:T(8,128)(2,1)S(1)} fusion(bf16[128,32,256]{2,1,0:T(8,128)(2,1)} %bitcast.183, f32[128]{0:T(128)S(1)} %fusion.94, bf16[256,8,32]{0,2,1:T(8,128)(2,1)S(1)} %get-tuple-element.237, s32[]{:T(128)S(6)} %select_n.28), kind=kOutput, calls=%fused_computation.4.clone.1 | convolution fusion | flops 67371008 | bytes 2376196 | tf_op jit(solution)/shard_map/while/body/eval_jaxpr/dot_general | solution.py:32
  127.5 4.0 %fusion.95 = bf16[128,32,32]{0,1,2:T(8,128)(2,1)S(1)} fusion(bf16[128,32,256]{2,1,0:T(8,128)(2,1)} %bitcast.183, f32[128]{0:T(128)S(1)} %fusion.94, bf16[256,8,32]{0,2,1:T(8,128)(2,1)S(1)} %get-tuple-element.237, s32[]{:T(128)S(6)} %select_n.28), kind=kOutput, calls=%fused_computation.4.clone.1 | convolution fusion | flops 67371008 | bytes 2376196 | tf_op jit(solution)/shard_map/while/body/eval_jaxpr/dot_general | solution.py:32
  135.2 4.0 %fusion.95 = bf16[128,32,32]{0,1,2:T(8,128)(2,1)S(1)} fusion(bf16[128,32,256]{2,1,0:T(8,128)(2,1)} %bitcast.183, f32[128]{0:T(128)S(1)} %fusion.94, bf16[256,8,32]{0,2,1:T(8,128)(2,1)S(1)} %get-tuple-element.237, s32[]{:T(128)S(6)} %select_n.28), kind=kOutput, calls=%fused_computation.4.clone.1 | convolution fusion | flops 67371008 | bytes 2376196 | tf_op jit(solution)/shard_map/while/body/eval_jaxpr/dot_general | solution.py:32
  142.8 4.0 %fusion.95 = bf16[128,32,32]{0,1,2:T(8,128)(2,1)S(1)} fusion(bf16[128,32,256]{2,1,0:T(8,128)(2,1)} %bitcast.183, f32[128]{0:T(128)S(1)} %fusion.94, bf16[256,8,32]{0,2,1:T(8,128)(2,1)S(1)} %get-tuple-element.237, s32[]{:T(128)S(6)} %select_n.28), kind=kOutput, calls=%fused_computation.4.clone.1 | convolution fusion | flops 67371008 | bytes 2376196 | tf_op jit(solution)/shard_map/while/body/eval_jaxpr/dot_general | solution.py:32
  150.5 4.0 %fusion.95 = bf16[128,32,32]{0,1,2:T(8,128)(2,1)S(1)} fusion(bf16[128,32,256]{2,1,0:T(8,128)(2,1)} %bitcast.183, f32[128]{0:T(128)S(1)} %fusion.94, bf16[256,8,32]{0,2,1:T(8,128)(2,1)S(1)} %get-tuple-element.237, s32[]{:T(128)S(6)} %select_n.28), kind=kOutput, calls=%fused_computation.4.clone.1 | convolution fusion | flops 67371008 | bytes 2376196 | tf_op jit(solution)/shard_map/while/body/eval_jaxpr/dot_general | solution.py:32
  158.1 4.0 %fusion.95 = bf16[128,32,32]{0,1,2:T(8,128)(2,1)S(1)} fusion(bf16[128,32,256]{2,1,0:T(8,128)(2,1)} %bitcast.183, f32[128]{0:T(128)S(1)} %fusion.94, bf16[256,8,32]{0,2,1:T(8,128)(2,1)S(1)} %get-tuple-element.237, s32[]{:T(128)S(6)} %select_n.28), kind=kOutput, calls=%fused_computation.4.clone.1 | convolution fusion | flops 67371008 | bytes 2376196 | tf_op jit(solution)/shard_map/while/body/eval_jaxpr/dot_general | solution.py:32
  165.7 4.0 %fusion.95 = bf16[128,32,32]{0,1,2:T(8,128)(2,1)S(1)} fusion(bf16[128,32,256]{2,1,0:T(8,128)(2,1)} %bitcast.183, f32[128]{0:T(128)S(1)} %fusion.94, bf16[256,8,32]{0,2,1:T(8,128)(2,1)S(1)} %get-tuple-element.237, s32[]{:T(128)S(6)} %select_n.28), kind=kOutput, calls=%fused_computation.4.clone.1 | convolution fusion | flops 67371008 | bytes 2376196 | tf_op jit(solution)/shard_map/while/body/eval_jaxpr/dot_general | solution.py:32
  172.9 19.5 %all_gather.11 = bf16[8,128,128]{2,0,1:T(8,128)(2,1)S(1)} all-gather(bf16[8,8,128]{2,0,1:T(8,128)(2,1)S(1)} %fusion.41), channel_id=1, replica_groups=mesh['groups'=2,'row'=16] {'row'}, dimensions={1}, use_global_device_ids=true | all-gather | bytes 278528 | tf_op jit(solution)/shard_map/all_gather | solution.py:83
  192.6 43.6 %while.21 = (s32[]{:T(128)}, bf16[16,128,256]{1,2,0:T(8,128)(2,1)S(1)}, bf16[16,128,1024]{2,1,0:T(8,128)(2,1)}, bf16[16,128]{1,0:T(8,128)(2,1)S(1)}, bf16[8,128,128]{1,2,0:T(8,128)(2,1)S(1)}, /*index=5*/s32[]{:T(128)}) while((s32[]{:T(128)}, bf16[16,128,256]{1,2,0:T(8,128)(2,1)S(1)}, bf16[16,128,1024]{2,1,0:T(8,128)(2,1)}, ...), condition=%wide.region_11.12_spmd, body=%wide.region_6.11_spmd.sunk | while | flops 27101052 | bytes 3877329 | solution.py:112
  237.2 27.9 %all_to_all.55 = bf16[16,128,256]{2,0,1:T(8,128)(2,1)S(1)} all-to-all(bf16[16,128,256]{2,0,1:T(8,128)(2,1)S(1)} %copy.58), channel_id=1, replica_groups=mesh['groups'=2,'row'=16] {'row'}, dimensions={1} | all-to-all | bytes 2097152 | tf_op jit(solution)/shard_map/all_to_all | solution.py:113
  (259 shorter events, 64.2 us)
Async XLA Ops:
  7.2 49.0 %copy-start = (bf16[64,1024]{1,0:T(8,128)(2,1)S(1)}, bf16[64,1024]{1,0:T(8,128)(2,1)}, u32[]{:S(2)}) copy-start(bf16[64,1024]{1,0:T(8,128)(2,1)} %param.22) | copy-start | bytes 393220
  7.2 3.9 %copy-start.8 = (s32[256,8]{0,1:T(8,128)S(1)}, s32[256,8]{0,1:T(8,128)}, u32[]{:S(2)}) copy-start(s32[256,8]{0,1:T(8,128)} %param.16) | copy-start | bytes 24580
  7.2 3.9 %copy-start.9 = (s32[8]{0:T(128)S(1)}, s32[8]{0:T(128)}, u32[]{:S(2)}) copy-start(s32[8]{0:T(128)} %param.17) | copy-start | bytes 100
  7.2 47.2 %copy-start.6 = (bf16[64,32]{0,1:T(8,128)(2,1)S(1)}, bf16[64,32]{0,1:T(8,128)(2,1)}, u32[]{:S(2)}) copy-start(bf16[64,32]{0,1:T(8,128)(2,1)} %param.18) | copy-start | bytes 12292
  7.2 92.4 %all-gather.2.cloned.1.call-start = ((), (), s32[]{:S(2)}) async-start(), calls=%async_computation.3 | async-start | bytes 8912896 | tf_op jit(solution)/shard_map/all_gather | solution.py:63
  11.1 88.5 %copy-start.7 = (bf16[64,32]{0,1:T(8,128)(2,1)S(1)}, bf16[64,32]{0,1:T(8,128)(2,1)}, u32[]{:S(2)}) copy-start(bf16[64,32]{0,1:T(8,128)(2,1)} %param.19) | copy-start | bytes 12292
  11.9 13.3 %all-to-all-start.1 = ((bf16[16,16,8]{1,2,0:T(8,128)(2,1)}), bf16[16,16,8]{1,2,0:T(8,128)(2,1)S(1)}, u32[]{:S(2)}, u32[]{:S(2)}) async-start(bf16[16,16,8]{1,2,0:T(8,128)(2,1)} %copy.54), calls=%async_computation.1 | async-start | bytes 65536 | tf_op jit(solution)/shard_map/all_to_all | solution.py:78
  25.1 30.7 %all-to-all-start = ((bf16[16,2,4096]{2,1,0:T(2,128)(2,1)}), bf16[16,2,4096]{2,1,0:T(2,128)(2,1)S(1)}, u32[]{:S(2)}, u32[]{:S(2)}) async-start(bf16[16,2,4096]{2,1,0:T(2,128)(2,1)} %reshape.98), calls=%async_computation | async-start | bytes 524288 | tf_op jit(solution)/shard_map/all_to_all | solution.py:77
  106.0 3.6 %copy-start.1 = (bf16[1024,128]{1,0:T(8,128)(2,1)S(1)}, bf16[1024,128]{1,0:T(8,128)(2,1)}, u32[]{:S(2)}) copy-start(bf16[1024,128]{1,0:T(8,128)(2,1)} %param.20) | copy-start | bytes 786436
  109.6 61.2 %copy-start.4 = (bf16[8,128,128]{2,1,0:T(8,128)(2,1)S(1)}, bf16[8,128,128]{2,1,0:T(8,128)(2,1)}, u32[]{:S(2)}) copy-start(bf16[8,128,128]{2,1,0:T(8,128)(2,1)} %param.15) | copy-start | bytes 786436
  109.6 62.8 %copy-start.10 = (bf16[128,8]{0,1:T(8,128)(2,1)S(1)}, bf16[128,8]{0,1:T(8,128)(2,1)}, u32[]{:S(2)}) copy-start(bf16[128,8]{0,1:T(8,128)(2,1)} %param.21) | copy-start | bytes 6148
  109.6 83.0 %copy-start.2 = (bf16[16,128,256]{1,2,0:T(8,128)(2,1)S(1)}, bf16[16,128,256]{1,2,0:T(8,128)(2,1)}, u32[]{:S(2)}) copy-start(bf16[16,128,256]{1,2,0:T(8,128)(2,1)} %custom-call.1) | copy-start | bytes 3145732
  172.0 20.6 %copy-start.3 = (bf16[8,128,128]{2,1,0:T(8,128)(2,1)}, bf16[8,128,128]{2,1,0:T(8,128)(2,1)S(1)}, u32[]{:S(2)}) copy-start(bf16[8,128,128]{2,1,0:T(8,128)(2,1)S(1)} %get-tuple-element.129) | copy-start | bytes 786436
  236.3 28.9 %copy-start.5 = (bf16[256,64]{0,1:T(8,128)(2,1)S(1)}, bf16[256,64]{0,1:T(8,128)(2,1)}, u32[]{:S(2)}) copy-start(bf16[256,64]{0,1:T(8,128)(2,1)} %param.23) | copy-start | bytes 98308
Sparse Core Ops, SparseCore 0:
  11.2 88.3 all-gather.1
where the time goes:
time: 275 us; the launch traced here: 274 us
  matrix products  75.5 us (27%)
  blocking collectives  72.2 us (26%)
  waiting for transfers between devices  43.9 us (16%)
  local copies, waits for them, and re-layouts  35.2 us (13%)
  loops' own time  16.7 us (6%)
  between operations  14.3 us (5%)
  starting transfers between devices  11.6 us (4%)
  other arithmetic  4.62 us (2%)
    all_gather x1, waiting for transfers between devices, on_device(): lax.all_gather((standardized_homologs, active_bfloat), 'row', axis=1, til...  40.1 us
    dot_general x8, matrix products, one_row(): jnp.dot(left_row.T, flat_right, preferred_element_type=jnp.float32)  31.8 us
    all_to_all x1, blocking collectives, on_device(): lax.all_to_all(gated_out, 'row', split_axis=1, concat_axis=0, tiled=True)  27.9 us
    all_gather x1, blocking collectives, on_device(): lax.all_gather((standardized_homologs, active_bfloat), 'row', axis=1, til...  24.8 us
    all_gather x1, blocking collectives, on_device(): bias_full = lax.all_gather(bias_local, 'row', axis=1, tiled=True)  19.5 us
    dynamic_slice x32, local copies, waits for them, and re-layouts, on_device(): gated_out = lax.map(attend, (projected_values, shifted_mask))  18.2 us
    another operation x1, loops' own time, opm_tile(): return lax.map(one_row, jnp.arange(left_rows.shape[1], dtype=jnp.int32))  15.7 us
    sub x32, matrix products, attend(): weights = jax.nn.softmax(logits, axis=-1).astype(jnp.bfloat16)  9.93 us
  transfers between devices with their start and end apart: 3, of which 2 were waited for; matrix products, arithmetic and copies ran while one was open for 3% of the time, Pallas kernels for 0%

commit v1 on v0

v1 whole, which is shorter than its diff:
```python
import functools
import math

import jax
import jax.numpy as jnp
from jax import lax
from jax.experimental import pallas as pl
from jax.experimental.pallas import tpu as pltpu
from jax.sharding import PartitionSpec as P

F32 = jnp.float32
BF16 = jnp.bfloat16
HEADS = 8
DIM = 32
FACTOR = 32
EPS = 1e-05
MESH = pl.DeviceIdType.MESH


def nn(a, b):
    return lax.dot_general(a, b, (((1,), (0,)), ((), ())), preferred_element_type=F32)


def nt(a, b):
    return lax.dot_general(a, b, (((1,), (1,)), ((), ())), preferred_element_type=F32)


def standardize(x):
    mean = jnp.mean(x, axis=-1, keepdims=True)
    centred = x - mean
    spread = jnp.mean(centred * centred, axis=-1, keepdims=True)
    return centred * lax.rsqrt(spread + EPS)


def iota(shape, dim):
    return lax.broadcasted_iota(jnp.int32, shape, dim)


def kernel(
    devices, seqs, own,
    h_ref, pair_ref, entry_ref, pad_ref, w1_ref, w2_ref, wt_ref, cg_ref, wq_ref, wo_ref,
    pair_out, out_ref,
    g_ref, n_ref, nf_ref, n2_ref, q_ref, a_ref, rs_ref, t_ref, lt_ref, live_ref, cap_ref,
    bias_ref, wf_ref, wp_ref, bd_ref, bv_ref,
    send_r, recv_r, send_l, recv_l, send_s, recv_s,
):
    half = seqs // 2
    rows = half * own
    length = devices * own
    ch = h_ref.shape[1]
    chips = devices // 2
    me = lax.axis_index("row")
    core = me % 2
    chip = me // 2
    odd = chip % 2
    pos = (1 - odd) * (chip // 2) + odd * (chips - 1 - chip // 2)

    def device_at(p):
        p = (p + chips) % chips
        hi = (2 * p) // chips
        c = (1 - hi) * 2 * p + hi * (2 * (chips - 1 - p) + 1)
        return 2 * c + core

    right, left, sibling = device_at(pos + 1), device_at(pos - 1), 2 * chip + 1 - core

    barrier = pltpu.get_barrier_semaphore()
    for other in (left, right, sibling):
        pl.semaphore_signal(barrier, inc=1, device_id={"row": other}, device_id_type=MESH)

    e0 = (iota((ch, 2 * ch), 0) == iota((ch, 2 * ch), 1)).astype(BF16)
    e1 = (iota((ch, 2 * ch), 0) + ch == iota((ch, 2 * ch), 1)).astype(BF16)
    piece = 256

    def prepare(k, _):
        at = pl.multiple_of(k * piece, piece)
        parts = []
        for hf in range(2):
            where = pl.ds(hf * rows + at, piece)
            normed = standardize(h_ref[where, :].astype(F32)).astype(BF16)
            n_ref[where, :] = normed
            nf_ref[where, :] = normed.astype(F32)
            parts.append(normed)
        g_ref[me, pl.ds(at, piece), :] = (nn(parts[0], e0) + nn(parts[1], e1)).astype(BF16)
        return 0

    lax.fori_loop(0, rows // piece, prepare, 0)
    diag = jnp.where(iota((own, own), 0) == iota((own, own), 1), pad_ref[...], 0).astype(F32).astype(BF16)
    live_own = nt(diag, entry_ref[...].astype(F32).astype(BF16))
    g_ref[me, rows : rows + 2 * own, :] = jnp.concatenate(
        [live_own[:, :half], live_own[:, half:]], axis=0
    ).astype(BF16)

    pl.semaphore_wait(barrier, 3)

    def move(origin, to, ssem, rsem):
        return pltpu.make_async_remote_copy(
            src_ref=g_ref.at[origin],
            dst_ref=g_ref.at[origin],
            send_sem=ssem,
            recv_sem=rsem,
            device_id={"row": to},
            device_id_type=MESH,
        )

    steps_r = chips // 2
    steps_l = chips - 1 - steps_r
    sent = []

    def send(origin, to, ssem, rsem):
        copy = move(origin, to, ssem, rsem)
        copy.start()
        sent.append(copy)

    send(me, right, send_r.at[0], recv_r.at[0])
    if steps_l:
        send(me, left, send_l.at[0], recv_l.at[0])
    send(me, sibling, send_s.at[0], recv_s.at[0])

    scale = 1.0 / math.sqrt(DIM)
    width = HEADS * DIM
    lanes = 2 * ch
    wk = wq_ref[:, width : 2 * width]
    wv = wq_ref[:, 2 * width : 3 * width]
    for hf, e in enumerate((e0, e1)):
        wkt = lax.dot_general(wk, e, (((0,), (0,)), ((), ())), preferred_element_type=F32)
        head = iota((width, lanes), 0) // DIM
        for hd in range(HEADS):
            bd_ref[hf, :, hd * lanes : (hd + 1) * lanes] = jnp.where(head == hd, wkt, 0.0).astype(BF16)
    zero = jnp.zeros((ch, width), F32)
    column = iota((lanes, width), 1) // DIM
    for hf in range(2):
        stacked = jnp.concatenate([wv.astype(F32), zero] if hf == 0 else [zero, wv.astype(F32)], axis=0)
        for hd in range(HEADS):
            bv_ref[hf, hd * lanes : (hd + 1) * lanes, :] = jnp.where(column == hd, stacked, 0.0).astype(BF16)
    wf_ref[...] = wt_ref[...].astype(F32)
    per = 128 // FACTOR
    for k in range(FACTOR // per):
        rowsets = [wf_ref[pl.ds(k * per + d, FACTOR, stride=FACTOR), :] for d in range(per)]
        wp_ref[:, k * 128 : (k + 1) * 128] = jnp.concatenate(rowsets, axis=0).T.astype(BF16)
    w2 = w2_ref[...]
    w2t = jnp.concatenate(
        [lax.dot_general(w2, e, (((0,), (0,)), ((), ())), preferred_element_type=F32) for e in (e0, e1)], axis=0
    ).astype(BF16)
    eye = (iota((own, HEADS), 0) == iota((own, HEADS), 1)).astype(BF16)
    cgt = nt(eye, cg_ref[...]).astype(BF16)
    w1 = w1_ref[...]
    for i in range(own):
        n_i = nf_ref[pl.ds(i, seqs, stride=own), :].astype(BF16)
        lt = lax.dot_general(w1, n_i, (((0,), (1,)), ((), ())), preferred_element_type=F32)
        lt_ref[i * FACTOR : (i + 1) * FACTOR, :] = (lt * live_own[i : i + 1, :]).astype(BF16)

    group = 256 // own

    def queries(k, _):
        at = pl.multiple_of(k * 256, 256)
        for hf in range(2):
            q = nn(n_ref[pl.ds(hf * rows + at, 256), :], wq_ref[:, :width]).astype(BF16)
            folded = nn(q, bd_ref[hf]) * scale
            for s in range(group):
                block = folded[s * own : (s + 1) * own]
                tall = jnp.concatenate([block[:, hd * lanes : (hd + 1) * lanes] for hd in range(HEADS)], axis=0)
                q_ref[k * group + s, hf * HEADS * own : (hf + 1) * HEADS * own, :] = tall.astype(BF16)
        return 0

    lax.fori_loop(0, rows // 256, queries, 0)

    for t in range(steps_r):
        origin = device_at(pos - 1 - t)
        move(origin, right, send_r.at[t], recv_r.at[t]).wait_recv()
        if t + 1 < steps_r:
            send(origin, right, send_r.at[t + 1], recv_r.at[t + 1])
        send(origin, sibling, send_s.at[1 + t], recv_s.at[1 + t])
        if t < steps_l:
            origin = device_at(pos + 1 + t)
            move(origin, left, send_l.at[t], recv_l.at[t]).wait_recv()
            if t + 1 < steps_l:
                send(origin, left, send_l.at[t + 1], recv_l.at[t + 1])
            send(origin, sibling, send_s.at[1 + steps_r + t], recv_s.at[1 + steps_r + t])
    for t in range(chips):
        origin = device_at(pos if t == 0 else (pos - t if t <= steps_r else pos + t - steps_r))
        origin = origin + 1 - 2 * core
        move(origin, sibling, send_s.at[t], recv_s.at[t]).wait_recv()
    for copy in sent:
        copy.wait_send()

    def relay(p, _):
        at = pl.ds(pl.multiple_of(p * 16, 16), 16)
        for c in range(chips):
            x = g_ref[2 * c, at, :].astype(F32)
            y = g_ref[2 * c + 1, at, :].astype(F32)
            n2_ref[2 * p, 16 * c : 16 * c + 16, :] = jnp.concatenate([x[:8], y[:8]], axis=0).astype(BF16)
            n2_ref[2 * p + 1, 16 * c : 16 * c + 16, :] = jnp.concatenate([x[8:], y[8:]], axis=0).astype(BF16)
        return 0

    lax.fori_loop(0, half // 2, relay, 0)

    live_b = live_own.astype(BF16)
    for jc in range(length // 128):
        js = slice(jc * 128, (jc + 1) * 128)
        masks = [g_ref[r, rows : rows + 2 * own, :].astype(F32) for r in range(jc * 16, (jc + 1) * 16)]
        for hf in range(2):
            tall = jnp.concatenate([m[hf * own : (hf + 1) * own] for m in masks], axis=0)
            live_ref[jc, hf * half : (hf + 1) * half, :] = tall.T
        live_j = live_ref[jc]
        cap_ref[jc] = jnp.where(live_j > 0, 3e38, -1000000000.0)
        inverse = 1.0 / jnp.maximum(nn(live_b, live_j.astype(BF16)), 1.0)

        def factor(s, _):
            block = nt(w2t, n2_ref[s, js, :])
            rs_ref[pl.ds(pl.multiple_of(s * 2 * FACTOR, 2 * FACTOR), 2 * FACTOR), :] = jnp.concatenate(
                [
                    block[:FACTOR] * live_ref[jc, pl.ds(s, 1), :],
                    block[FACTOR:] * live_ref[jc, pl.ds(half + s, 1), :],
                ],
                axis=0,
            )
            return 0

        lax.fori_loop(0, half, factor, 0, unroll=4)

        def outer(k, _):
            columns = []
            for d in range(2):
                columns.append(
                    jnp.concatenate(
                        [
                            rs_ref[pl.ds(hf * FACTOR + 2 * k + d, half, stride=2 * FACTOR), :].astype(BF16)
                            for hf in range(2)
                        ],
                        axis=0,
                    )
                )
            prod = nn(lt_ref[...], jnp.concatenate(columns, axis=1))
            for i in range(own):
                for d in range(2):
                    tile = prod[i * FACTOR : (i + 1) * FACTOR, d * 128 : (d + 1) * 128] * inverse[i : i + 1, :]
                    at = pl.multiple_of((2 * k + d) * FACTOR, FACTOR)
                    t_ref[i, pl.ds(at, FACTOR), :] = tile.astype(BF16)
            return 0

        lax.fori_loop(0, FACTOR // 2, outer, 0)

        for i in range(own):
            update = nn(wp_ref[...], t_ref[i]).T
            pair = (pair_ref[i, js, :].astype(F32) + update).astype(BF16)
            pair_out[i, js, :] = pair
            normed = standardize(pair.astype(F32)).astype(BF16)
            bias_ref[jc, pl.ds(i, HEADS, stride=own), :] = nt(cgt, normed).astype(BF16).astype(F32)

    def cap_row(s):
        return jnp.concatenate([cap_ref[jc, pl.ds(s, 1), :] for jc in range(length // 128)], axis=1)

    def attend(p, _):
        results = []
        for k in range(2):
            s = 2 * p + k
            keys = n2_ref[s]
            logits = nt(q_ref[s], keys)
            bias = jnp.concatenate([bias_ref[jc] for jc in range(length // 128)], axis=1)
            m = HEADS * own
            logits = jnp.concatenate(
                [
                    jnp.minimum(logits[:m] + bias, cap_row(s)),
                    jnp.minimum(logits[m:] + bias, cap_row(half + s)),
                ],
                axis=0,
            )
            top = jnp.max(logits, axis=1, keepdims=True)
            weights = jnp.exp(logits - top)
            total = jnp.sum(weights, axis=1, keepdims=True)
            results.append(nn(weights.astype(BF16), keys) * (1.0 / total))
        at = pl.ds(pl.multiple_of(p * 2 * own, 2 * own), 2 * own)
        for hf in range(2):
            for hd in range(HEADS):
                start = (hf * HEADS + hd) * own
                tile = jnp.concatenate([r[start : start + own] for r in results], axis=0)
                a_ref[hf, at, hd * lanes : (hd + 1) * lanes] = tile.astype(BF16)
        return 0

    lax.fori_loop(0, half // 2, attend, 0)

    def finish(k, _):
        at = pl.multiple_of(k * 256, 256)
        for hf in range(2):
            where = pl.ds(hf * rows + at, 256)
            attended = nn(a_ref[hf, pl.ds(at, 256), :], bv_ref[hf])
            gate = nn(n_ref[where, :], wq_ref[:, 3 * width :]).astype(BF16).astype(F32)
            gated = (attended * jax.nn.sigmoid(gate)).astype(BF16)
            increment = nn(gated, wo_ref[...])
            out_ref[where, :] = (h_ref[where, :].astype(F32) + increment).astype(BF16)
        return 0

    lax.fori_loop(0, rows // 256, finish, 0)


def on_device(devices, homolog, coupling, entry, nonpadding, w1, w2, wt, cg, wq, wo):
    seqs, own, ch = homolog.shape
    half = seqs // 2
    rows = half * own
    length = coupling.shape[1]
    chips = devices // 2
    lanes = 2 * ch
    dma = pltpu.SemaphoreType.DMA
    vmem = pl.BlockSpec(memory_space=pltpu.VMEM)
    pair_output, refreshed = pl.pallas_call(
        functools.partial(kernel, devices, seqs, own),
        out_shape=(
            jax.ShapeDtypeStruct(coupling.shape, BF16),
            jax.ShapeDtypeStruct((seqs * own, ch), BF16),
        ),
        in_specs=[vmem] * 10,
        out_specs=(vmem, vmem),
        scratch_shapes=[
            pltpu.VMEM((devices, rows + 2 * own, lanes), BF16),
            pltpu.VMEM((2 * rows, ch), BF16),
            pltpu.VMEM((2 * rows, ch), F32),
            pltpu.VMEM((half, length, lanes), BF16),
            pltpu.VMEM((half, 2 * HEADS * own, lanes), BF16),
            pltpu.VMEM((2, rows, HEADS * lanes), BF16),
            pltpu.VMEM((half * 2 * FACTOR, 128), F32),
            pltpu.VMEM((own, FACTOR * FACTOR, 128), BF16),
            pltpu.VMEM((own * FACTOR, seqs), BF16),
            pltpu.VMEM((length // 128, seqs, 128), F32),
            pltpu.VMEM((length // 128, seqs, 128), F32),
            pltpu.VMEM((length // 128, HEADS * own, 128), F32),
            pltpu.VMEM((FACTOR * FACTOR, 128), F32),
            pltpu.VMEM((128, FACTOR * FACTOR), BF16),
            pltpu.VMEM((2, HEADS * DIM, HEADS * lanes), BF16),
            pltpu.VMEM((2, HEADS * lanes, HEADS * DIM), BF16),
            dma((chips,)), dma((chips,)), dma((chips,)), dma((chips,)), dma((chips,)), dma((chips,)),
        ],
        compiler_params=pltpu.CompilerParams(
            collective_id=0, has_side_effects=True, vmem_limit_bytes=62 * 1024 * 1024
        ),
    )(
        homolog.reshape(seqs * own, ch), coupling, entry, nonpadding.reshape(1, own),
        w1, w2, wt, cg, wq, wo,
    )
    return pair_output, refreshed.reshape(seqs, own, ch)


def solution(mesh):
    return jax.shard_map(
        functools.partial(on_device, mesh.shape["row"]),
        mesh=mesh,
        in_specs=(
            P("groups", "row", None),
            P(("groups", "row"), None, None),
            P("groups", "row"),
            P(("groups", "row")),
            P(), P(), P(), P(), P(), P(),
        ),
        out_specs=(P(("groups", "row"), None, None), P("groups", "row", None)),
        check_vma=False,
    )
```

time: 275 us -> 106 us (0.39)
  Pallas kernels: 0 us -> 94.1 us
  matrix products: 75.5 us -> 0 us
  blocking collectives: 72.2 us -> 0 us
  waiting for transfers between devices: 43.9 us -> 0 us
  local copies, waits for them, and re-layouts: 35.2 us -> 11 us
  loops' own time: 16.7 us -> 0 us
  between operations: 14.3 us -> 0.66 us
  starting transfers between devices: 11.6 us -> 0 us
  other arithmetic: 4.62 us -> 0 us
    pallas_call x0 -> x1, Pallas kernels: none -> 94.1 us  [on_device(): pl.pallas_call(functools.partial(kernel, devices, seqs, own), out_shape=(...]
    dot_general x93 -> x0, matrix products: 65.6 us -> none  [the longest x8 31.8 us: one_row(): jnp.dot(left_row.T, flat_right, preferred_element_type=jnp.float32)]
    all_gather x2 -> x0, blocking collectives: 44.3 us -> none  [the longest x1 24.8 us: on_device(): lax.all_gather((standardized_homologs, active_bfloat), 'row', axis=1, til...]
    all_gather x1 -> x0, waiting for transfers between devices: 40.1 us -> none  [on_device(): lax.all_gather((standardized_homologs, active_bfloat), 'row', axis=1, til...]
    all_to_all x1 -> x0, blocking collectives: 27.9 us -> none  [on_device(): lax.all_to_all(gated_out, 'row', split_axis=1, concat_axis=0, tiled=True)]
    dynamic_slice x40 -> x0, local copies, waits for them, and re-layouts: 22.9 us -> none  [the longest x32 18.2 us: on_device(): gated_out = lax.map(attend, (projected_values, shifted_mask))]
    another operation x2 -> x0, loops' own time: 16.7 us -> none  [the longest x1 15.7 us: opm_tile(): return lax.map(one_row, jnp.arange(left_rows.shape[1], dtype=jnp.int32))]
    all_to_all x2 -> x0, starting transfers between devices: 11.6 us -> none  [the longest x1 7.35 us: on_device(): lax.all_to_all(active_bfloat, 'row', split_axis=0, concat_axis=1, tiled=T...]
  transfers between devices with their start and end apart: 3 -> 0, of which waited for: 2 -> 0; matrix products, arithmetic and copies ran while one was open for 3% -> 0% of each run, Pallas kernels for 0% -> 0%
where the time goes in v1:
time: 106 us
  Pallas kernels  94.1 us (89%)
  local copies, waits for them, and re-layouts  11 us (10%)
    pallas_call x1, Pallas kernels, on_device(): pl.pallas_call(functools.partial(kernel, devices, seqs, own), out_shape=(...  94.1 us
    unnamed x12, local copies, waits for them, and re-layouts  11 us

profile of v1, /device:TPU:1, one launch (start us, length us, event | category | flops | bytes accessed | tf_op | source)
XLA Modules:
  0.0 105.7 jit_solution(1424011832024979392)
XLA Ops:
  0.6 0.0 copy-start
  0.6 1.4 %copy.14.w1_ref = bf16[64,32]{1,0:T(8,128)(2,1)} copy(bf16[64,32]{0,1:T(8,128)(2,1)} %param.14) | data formatting | bytes 8192 | tf_op args[4]
  2.1 1.4 %copy.15.w2_ref = bf16[64,32]{1,0:T(8,128)(2,1)} copy(bf16[64,32]{0,1:T(8,128)(2,1)} %param.15) | data formatting | bytes 8192 | tf_op args[5]
  3.4 1.4 %copy.16.cg_ref = bf16[128,8]{1,0:T(8,128)(2,1)} copy(bf16[128,8]{0,1:T(8,128)(2,1)} %param.17) | data formatting | bytes 4096 | tf_op args[7]
  4.8 1.5 %copy.17.wo_ref = bf16[256,64]{1,0:T(8,128)(2,1)} copy(bf16[256,64]{0,1:T(8,128)(2,1)} %param.19) | data formatting | bytes 65536 | tf_op args[9]
  6.3 1.5 %copy.13.entry_ref = s32[256,8]{1,0:T(8,128)} copy(s32[256,8]{0,1:T(8,128)} %param.12) | data formatting | bytes 16384 | tf_op args[2]
  7.8 0.0 copy-done
  7.8 1.1 %copy.12 = bf16[256,8,64]{2,1,0:T(8,128)(2,1)} copy(bf16[256,8,64]{0,2,1:T(8,128)(2,1)S(1)} %copy-done) | data formatting | bytes 524288 | tf_op args[0]
  8.9 94.1 %shard_map.113 = (bf16[8,128,128]{2,1,0:T(8,128)(2,1)}, bf16[2048,64]{1,0:T(8,128)(2,1)}) custom-call(bf16[2048,64]{1,0:T(8,128)(2,1)} %bitcast.3, bf16[8,128,128]{2,1,0:T(8,128)(2,1)} %pair_ref.1, s32[256,8]{1,0:T(8,128)} %copy.13.entry_ref, s32[1,8]{1,0:T(1,128)} %bitcast.5, bf16[64,32]{1,0:T(8,128)(2,1)} %copy.14.w1_ref, bf16[64,32]{1,0:T(8,128)(2,1)} %copy.15.w2_ref, ...), custom_call_target="tpu_custom_call" | custom-call | tf_op jit(solution)/shard_map/pallas_call | solution.py:305
  103.0 0.0 copy-start.1
  103.0 2.1 %copy.18 = bf16[256,8,64]{0,2,1:T(8,128)(2,1)} copy(bf16[256,8,64]{2,1,0:T(8,128)(2,1)} %bitcast.4) | data formatting | bytes 524288
  105.0 0.0 copy-done.1
  105.0 0.7 copy.20
Async XLA Ops:
  0.6 7.2 %copy-start = (bf16[256,8,64]{0,2,1:T(8,128)(2,1)S(1)}, bf16[256,8,64]{0,2,1:T(8,128)(2,1)}, u32[]{:S(2)}) copy-start(bf16[256,8,64]{0,2,1:T(8,128)(2,1)} %param.10) | copy-start | bytes 786436
  103.0 2.1 %copy-start.1 = (bf16[8,128,128]{2,1,0:T(8,128)(2,1)S(1)}, bf16[8,128,128]{2,1,0:T(8,128)(2,1)}, u32[]{:S(2)}) copy-start(bf16[8,128,128]{2,1,0:T(8,128)(2,1)} %get-tuple-element.10) | copy-start | bytes 786436

commit v2 on v1

--- a/solution.py
+++ b/solution.py
@@ -14,6 +14,7 @@
 DIM = 32
 FACTOR = 32
 EPS = 1e-05
+PIECES = 4
 MESH = pl.DeviceIdType.MESH
 
 
@@ -40,7 +41,7 @@
     devices, seqs, own,
     h_ref, pair_ref, entry_ref, pad_ref, w1_ref, w2_ref, wt_ref, cg_ref, wq_ref, wo_ref,
     pair_out, out_ref,
-    g_ref, n_ref, nf_ref, n2_ref, q_ref, a_ref, rs_ref, t_ref, lt_ref, live_ref, cap_ref,
+    g_ref, n_ref, nf_ref, n2_ref, n2t_ref, q_ref, a_ref, rs_ref, t_ref, lt_ref, live_ref, cap_ref,
     bias_ref, wf_ref, wp_ref, bd_ref, bv_ref,
     send_r, recv_r, send_l, recv_l, send_s, recv_s,
 ):
@@ -48,6 +49,8 @@
     rows = half * own
     length = devices * own
     ch = h_ref.shape[1]
+    head = 2 * own
+    flip = length == 128
     chips = devices // 2
     me = lax.axis_index("row")
     core = me % 2
@@ -80,41 +83,50 @@
             n_ref[where, :] = normed
             nf_ref[where, :] = normed.astype(F32)
             parts.append(normed)
-        g_ref[me, pl.ds(at, piece), :] = (nn(parts[0], e0) + nn(parts[1], e1)).astype(BF16)
+        g_ref[me, pl.ds(head + at, piece), :] = (nn(parts[0], e0) + nn(parts[1], e1)).astype(BF16)
         return 0
 
     lax.fori_loop(0, rows // piece, prepare, 0)
     diag = jnp.where(iota((own, own), 0) == iota((own, own), 1), pad_ref[...], 0).astype(F32).astype(BF16)
     live_own = nt(diag, entry_ref[...].astype(F32).astype(BF16))
-    g_ref[me, rows : rows + 2 * own, :] = jnp.concatenate(
+    g_ref[me, :head, :] = jnp.concatenate(
         [live_own[:, :half], live_own[:, half:]], axis=0
     ).astype(BF16)
 
     pl.semaphore_wait(barrier, 3)
 
-    def move(origin, to, ssem, rsem):
+    hops = chips // 2
+    size = rows // PIECES
+
+    def move(origin, to, c, ssem, rsem):
+        span = pl.ds(0, size + head) if c == 0 else pl.ds(head + c * size, size)
         return pltpu.make_async_remote_copy(
-            src_ref=g_ref.at[origin],
-            dst_ref=g_ref.at[origin],
+            src_ref=g_ref.at[origin, span],
+            dst_ref=g_ref.at[origin, span],
             send_sem=ssem,
             recv_sem=rsem,
             device_id={"row": to},
             device_id_type=MESH,
         )
 
-    steps_r = chips // 2
-    steps_l = chips - 1 - steps_r
     sent = []
 
-    def send(origin, to, ssem, rsem):
-        copy = move(origin, to, ssem, rsem)
+    def send(*what):
+        copy = move(*what)
         copy.start()
         sent.append(copy)
 
-    send(me, right, send_r.at[0], recv_r.at[0])
-    if steps_l:
-        send(me, left, send_l.at[0], recv_l.at[0])
-    send(me, sibling, send_s.at[0], recv_s.at[0])
+    def reach(c):
+        return hops - c % 2, hops - 1 + c % 2
+
+    for c in range(PIECES):
+        far_r, far_l = reach(c)
+        if far_r:
+            send(me, right, c, send_r.at[0, c], recv_r.at[0, c])
+        if far_l:
+            send(me, left, c, send_l.at[0, c], recv_l.at[0, c])
+    for c in range(PIECES):
+        send(me, sibling, c, send_s.at[0, c], recv_s.at[0, c])
 
     scale = 1.0 / math.sqrt(DIM)
     width = HEADS * DIM
@@ -123,9 +135,9 @@
     wv = wq_ref[:, 2 * width : 3 * width]
     for hf, e in enumerate((e0, e1)):
         wkt = lax.dot_general(wk, e, (((0,), (0,)), ((), ())), preferred_element_type=F32)
-        head = iota((width, lanes), 0) // DIM
+        owner = iota((width, lanes), 0) // DIM
         for hd in range(HEADS):
-            bd_ref[hf, :, hd * lanes : (hd + 1) * lanes] = jnp.where(head == hd, wkt, 0.0).astype(BF16)
+            bd_ref[hf, :, hd * lanes : (hd + 1) * lanes] = jnp.where(owner == hd, wkt, 0.0).astype(BF16)
     zero = jnp.zeros((ch, width), F32)
     column = iota((lanes, width), 1) // DIM
     for hf in range(2):
@@ -164,59 +176,80 @@
 
     lax.fori_loop(0, rows // 256, queries, 0)
 
-    for t in range(steps_r):
-        origin = device_at(pos - 1 - t)
-        move(origin, right, send_r.at[t], recv_r.at[t]).wait_recv()
-        if t + 1 < steps_r:
-            send(origin, right, send_r.at[t + 1], recv_r.at[t + 1])
-        send(origin, sibling, send_s.at[1 + t], recv_s.at[1 + t])
-        if t < steps_l:
-            origin = device_at(pos + 1 + t)
-            move(origin, left, send_l.at[t], recv_l.at[t]).wait_recv()
-            if t + 1 < steps_l:
-                send(origin, left, send_l.at[t + 1], recv_l.at[t + 1])
-            send(origin, sibling, send_s.at[1 + steps_r + t], recv_s.at[1 + steps_r + t])
-    for t in range(chips):
-        origin = device_at(pos if t == 0 else (pos - t if t <= steps_r else pos + t - steps_r))
-        origin = origin + 1 - 2 * core
-        move(origin, sibling, send_s.at[t], recv_s.at[t]).wait_recv()
+    def read_masks():
+        for jc in range(length // 128):
+            masks = [g_ref[r, :head, :].astype(F32) for r in range(jc * 16, (jc + 1) * 16)]
+            for hf in range(2):
+                tall = jnp.concatenate([m[hf * own : (hf + 1) * own] for m in masks], axis=0)
+                live_ref[jc, hf * half : (hf + 1) * half, :] = tall.T
+
+    def factor(s, block, jc):
+        rs_ref[pl.ds(pl.multiple_of(s * 2 * FACTOR, 2 * FACTOR), 2 * FACTOR), :] = jnp.concatenate(
+            [
+                block[:FACTOR] * live_ref[jc, pl.ds(s, 1), :],
+                block[FACTOR:] * live_ref[jc, pl.ds(half + s, 1), :],
+            ],
+            axis=0,
+        )
+
+    def relay(p, _):
+        at = pl.ds(pl.multiple_of(head + p * 16, 16), 16)
+        tiles = [g_ref[r, at, :].astype(F32) for r in range(devices)]
+        for k in range(2):
+            keys = jnp.concatenate([x[k * own : (k + 1) * own] for x in tiles], axis=0).astype(BF16)
+            n2_ref[2 * p + k] = keys
+            if flip:
+                turned = keys.T
+                n2t_ref[2 * p + k] = turned
+                factor(2 * p + k, nn(w2t, turned), 0)
+        return 0
+
+    def work(c):
+        far_r, far_l = reach(c)
+        arrivals = [(pos, 0)] + [(pos - 1 - t, 1 + t) for t in range(far_r)]
+        arrivals += [(pos + 1 + t, 1 + hops + t) for t in range(far_l)]
+        for where, slot in arrivals:
+            origin = device_at(where) + 1 - 2 * core
+            move(origin, sibling, c, send_s.at[slot, c], recv_s.at[slot, c]).wait_recv()
+        if c == 0:
+            read_masks()
+        pairs = half // 2 // PIECES
+        lax.fori_loop(c * pairs, (c + 1) * pairs, relay, 0, unroll=2)
+
+    for t in range(hops):
+        ahead, back = device_at(pos - 1 - t), device_at(pos + 1 + t)
+        for c in range(PIECES):
+            far_r, far_l = reach(c)
+            if t < far_r:
+                move(ahead, right, c, send_r.at[t, c], recv_r.at[t, c]).wait_recv()
+                if t + 1 < far_r:
+                    send(ahead, right, c, send_r.at[t + 1, c], recv_r.at[t + 1, c])
+                send(ahead, sibling, c, send_s.at[1 + t, c], recv_s.at[1 + t, c])
+            if t < far_l:
+                move(back, left, c, send_l.at[t, c], recv_l.at[t, c]).wait_recv()
+                if t + 1 < far_l:
+                    send(back, left, c, send_l.at[t + 1, c], recv_l.at[t + 1, c])
+                send(back, sibling, c, send_s.at[1 + hops + t, c], recv_s.at[1 + hops + t, c])
+            if t == hops - 1 and c > 0:
+                work(c - 1)
+    work(PIECES - 1)
     for copy in sent:
         copy.wait_send()
-
-    def relay(p, _):
-        at = pl.ds(pl.multiple_of(p * 16, 16), 16)
-        for c in range(chips):
-            x = g_ref[2 * c, at, :].astype(F32)
-            y = g_ref[2 * c + 1, at, :].astype(F32)
-            n2_ref[2 * p, 16 * c : 16 * c + 16, :] = jnp.concatenate([x[:8], y[:8]], axis=0).astype(BF16)
-            n2_ref[2 * p + 1, 16 * c : 16 * c + 16, :] = jnp.concatenate([x[8:], y[8:]], axis=0).astype(BF16)
-        return 0
-
-    lax.fori_loop(0, half // 2, relay, 0)
 
     live_b = live_own.astype(BF16)
     for jc in range(length // 128):
         js = slice(jc * 128, (jc + 1) * 128)
-        masks = [g_ref[r, rows : rows + 2 * own, :].astype(F32) for r in range(jc * 16, (jc + 1) * 16)]
-        for hf in range(2):
-            tall = jnp.concatenate([m[hf * own : (hf + 1) * own] for m in masks], axis=0)
-            live_ref[jc, hf * half : (hf + 1) * half, :] = tall.T
         live_j = live_ref[jc]
         cap_ref[jc] = jnp.where(live_j > 0, 3e38, -1000000000.0)
         inverse = 1.0 / jnp.maximum(nn(live_b, live_j.astype(BF16)), 1.0)
 
-        def factor(s, _):
-            block = nt(w2t, n2_ref[s, js, :])
-            rs_ref[pl.ds(pl.multiple_of(s * 2 * FACTOR, 2 * FACTOR), 2 * FACTOR), :] = jnp.concatenate(
-                [
-                    block[:FACTOR] * live_ref[jc, pl.ds(s, 1), :],
-                    block[FACTOR:] * live_ref[jc, pl.ds(half + s, 1), :],
-                ],
-                axis=0,
-            )
-            return 0
-
-        lax.fori_loop(0, half, factor, 0, unroll=4)
+        if not flip:
+
+            def late(s, _):
+                factor(s, nt(w2t, n2_ref[s, js, :]), jc)
+                return 0
+
+            lax.fori_loop(0, half, late, 0, unroll=4)
 
         def outer(k, _):
             columns = []
@@ -250,12 +283,14 @@
     def cap_row(s):
         return jnp.concatenate([cap_ref[jc, pl.ds(s, 1), :] for jc in range(length // 128)], axis=1)
 
+    ones = jnp.ones((length, lanes), BF16)
+
     def attend(p, _):
         results = []
         for k in range(2):
             s = 2 * p + k
             keys = n2_ref[s]
-            logits = nt(q_ref[s], keys)
+            logits = nn(q_ref[s], n2t_ref[s]) if flip else nt(q_ref[s], keys)
             bias = jnp.concatenate([bias_ref[jc] for jc in range(length // 128)], axis=1)
             m = HEADS * own
             logits = jnp.concatenate(
@@ -267,8 +302,8 @@
             )
             top = jnp.max(logits, axis=1, keepdims=True)
             weights = jnp.exp(logits - top)
-            total = jnp.sum(weights, axis=1, keepdims=True)
-            results.append(nn(weights.astype(BF16), keys) * (1.0 / total))
+            mixed = nn(weights.astype(BF16), jnp.concatenate([keys, ones], axis=1))
+            results.append(mixed[:, :lanes] / mixed[:, lanes:])
         at = pl.ds(pl.multiple_of(p * 2 * own, 2 * own), 2 * own)
         for hf in range(2):
             for hd in range(HEADS):
@@ -277,7 +312,7 @@
                 a_ref[hf, at, hd * lanes : (hd + 1) * lanes] = tile.astype(BF16)
         return 0
 
-    lax.fori_loop(0, half // 2, attend, 0)
+    lax.fori_loop(0, half // 2, attend, 0, unroll=4 if flip else 1)
 
     def finish(k, _):
         at = pl.multiple_of(k * 256, 256)
@@ -315,6 +350,7 @@
             pltpu.VMEM((2 * rows, ch), BF16),
             pltpu.VMEM((2 * rows, ch), F32),
             pltpu.VMEM((half, length, lanes), BF16),
+            pltpu.VMEM((half if length == 128 else 1, lanes, 128), BF16),
             pltpu.VMEM((half, 2 * HEADS * own, lanes), BF16),
             pltpu.VMEM((2, rows, HEADS * lanes), BF16),
             pltpu.VMEM((half * 2 * FACTOR, 128), F32),
@@ -327,7 +363,8 @@
             pltpu.VMEM((128, FACTOR * FACTOR), BF16),
             pltpu.VMEM((2, HEADS * DIM, HEADS * lanes), BF16),
             pltpu.VMEM((2, HEADS * lanes, HEADS * DIM), BF16),
-            dma((chips,)), dma((chips,)), dma((chips,)), dma((chips,)), dma((chips,)), dma((chips,)),
+            dma((chips, PIECES)), dma((chips, PIECES)), dma((chips, PIECES)), dma((chips, PIECES)),
+            dma((chips + 1, PIECES)), dma((chips + 1, PIECES)),
         ],
         compiler_params=pltpu.CompilerParams(
             collective_id=0, has_side_effects=True, vmem_limit_bytes=62 * 1024 * 1024

time: 106 us -> 79.7 us (0.75)
  Pallas kernels: 94.1 us -> 67.7 us
    pallas_call x1, Pallas kernels: 94.1 us -> 67.7 us  [on_device(): pl.pallas_call(functools.partial(kernel, devices, seqs, own), out_shape=(...]
where the time goes in v2:
time: 79.7 us; the launch traced here: 79.4 us
  Pallas kernels  67.7 us (85%)
  local copies, waits for them, and re-layouts  11 us (14%)
    pallas_call x1, Pallas kernels, on_device(): pl.pallas_call(functools.partial(kernel, devices, seqs, own), out_shape=(...  67.7 us
    unnamed x12, local copies, waits for them, and re-layouts  11 us

profile of v2, /device:TPU:1, one launch (start us, length us, event | category | flops | bytes accessed | tf_op | source)
XLA Modules:
  0.0 79.4 jit_solution(2187406089477144802)
XLA Ops:
  0.6 0.0 copy-start
  0.6 1.4 %copy.14.w1_ref = bf16[64,32]{1,0:T(8,128)(2,1)} copy(bf16[64,32]{0,1:T(8,128)(2,1)} %param.14) | data formatting | bytes 8192 | tf_op args[4]
  2.1 1.4 %copy.15.w2_ref = bf16[64,32]{1,0:T(8,128)(2,1)} copy(bf16[64,32]{0,1:T(8,128)(2,1)} %param.15) | data formatting | bytes 8192 | tf_op args[5]
  3.4 1.4 %copy.16.cg_ref = bf16[128,8]{1,0:T(8,128)(2,1)} copy(bf16[128,8]{0,1:T(8,128)(2,1)} %param.17) | data formatting | bytes 4096 | tf_op args[7]
  4.8 1.5 %copy.17.wo_ref = bf16[256,64]{1,0:T(8,128)(2,1)} copy(bf16[256,64]{0,1:T(8,128)(2,1)} %param.19) | data formatting | bytes 65536 | tf_op args[9]
  6.3 1.5 %copy.13.entry_ref = s32[256,8]{1,0:T(8,128)} copy(s32[256,8]{0,1:T(8,128)} %param.12) | data formatting | bytes 16384 | tf_op args[2]
  7.8 0.0 copy-done
  7.8 1.1 %copy.12 = bf16[256,8,64]{2,1,0:T(8,128)(2,1)} copy(bf16[256,8,64]{0,2,1:T(8,128)(2,1)S(1)} %copy-done) | data formatting | bytes 524288 | tf_op args[0]
  8.9 67.7 %shard_map.113 = (bf16[8,128,128]{2,1,0:T(8,128)(2,1)}, bf16[2048,64]{1,0:T(8,128)(2,1)}) custom-call(bf16[2048,64]{1,0:T(8,128)(2,1)} %bitcast.3, bf16[8,128,128]{2,1,0:T(8,128)(2,1)} %pair_ref.1, s32[256,8]{1,0:T(8,128)} %copy.13.entry_ref, s32[1,8]{1,0:T(1,128)} %bitcast.5, bf16[64,32]{1,0:T(8,128)(2,1)} %copy.14.w1_ref, bf16[64,32]{1,0:T(8,128)(2,1)} %copy.15.w2_ref, ...), custom_call_target="tpu_custom_call" | custom-call | tf_op jit(solution)/shard_map/pallas_call | solution.py:340
  76.6 0.0 copy-start.1
  76.6 2.1 %copy.18 = bf16[256,8,64]{0,2,1:T(8,128)(2,1)} copy(bf16[256,8,64]{2,1,0:T(8,128)(2,1)} %bitcast.4) | data formatting | bytes 524288
  78.7 0.0 copy-done.1
  78.7 0.7 copy.20
Async XLA Ops:
  0.6 7.2 %copy-start = (bf16[256,8,64]{0,2,1:T(8,128)(2,1)S(1)}, bf16[256,8,64]{0,2,1:T(8,128)(2,1)}, u32[]{:S(2)}) copy-start(bf16[256,8,64]{0,2,1:T(8,128)(2,1)} %param.10) | copy-start | bytes 786436
  76.6 2.1 %copy-start.1 = (bf16[8,128,128]{2,1,0:T(8,128)(2,1)S(1)}, bf16[8,128,128]{2,1,0:T(8,128)(2,1)}, u32[]{:S(2)}) copy-start(bf16[8,128,128]{2,1,0:T(8,128)(2,1)} %get-tuple-element.10) | copy-start | bytes 786436

commit v3 on v2

--- a/solution.py
+++ b/solution.py
@@ -88,7 +88,7 @@
 
     lax.fori_loop(0, rows // piece, prepare, 0)
     diag = jnp.where(iota((own, own), 0) == iota((own, own), 1), pad_ref[...], 0).astype(F32).astype(BF16)
-    live_own = nt(diag, entry_ref[...].astype(F32).astype(BF16))
+    live_own = nn(diag, entry_ref[...].astype(F32).astype(BF16))
     g_ref[me, :head, :] = jnp.concatenate(
         [live_own[:, :half], live_own[:, half:]], axis=0
     ).astype(BF16)
@@ -151,14 +151,13 @@
         wp_ref[:, k * 128 : (k + 1) * 128] = jnp.concatenate(rowsets, axis=0).T.astype(BF16)
     w2 = w2_ref[...]
     w2t = jnp.concatenate(
-        [lax.dot_general(w2, e, (((0,), (0,)), ((), ())), preferred_element_type=F32) for e in (e0, e1)], axis=0
+        [nn(w2, e) for e in (e0, e1)], axis=0
     ).astype(BF16)
-    eye = (iota((own, HEADS), 0) == iota((own, HEADS), 1)).astype(BF16)
-    cgt = nt(eye, cg_ref[...]).astype(BF16)
+    cgt = cg_ref[...]
     w1 = w1_ref[...]
     for i in range(own):
         n_i = nf_ref[pl.ds(i, seqs, stride=own), :].astype(BF16)
-        lt = lax.dot_general(w1, n_i, (((0,), (1,)), ((), ())), preferred_element_type=F32)
+        lt = nt(w1, n_i)
         lt_ref[i * FACTOR : (i + 1) * FACTOR, :] = (lt * live_own[i : i + 1, :]).astype(BF16)
 
     group = 256 // own
@@ -312,7 +311,7 @@
                 a_ref[hf, at, hd * lanes : (hd + 1) * lanes] = tile.astype(BF16)
         return 0
 
-    lax.fori_loop(0, half // 2, attend, 0, unroll=4 if flip else 1)
+    lax.fori_loop(0, half // 2, attend, 0, unroll=8 if flip else 1)
 
     def finish(k, _):
         at = pl.multiple_of(k * 256, 256)
@@ -321,7 +320,7 @@
             attended = nn(a_ref[hf, pl.ds(at, 256), :], bv_ref[hf])
             gate = nn(n_ref[where, :], wq_ref[:, 3 * width :]).astype(BF16).astype(F32)
             gated = (attended * jax.nn.sigmoid(gate)).astype(BF16)
-            increment = nn(gated, wo_ref[...])
+            increment = nt(gated, wo_ref[...])
             out_ref[where, :] = (h_ref[where, :].astype(F32) + increment).astype(BF16)
         return 0
 
@@ -370,8 +369,8 @@
             collective_id=0, has_side_effects=True, vmem_limit_bytes=62 * 1024 * 1024
         ),
     )(
-        homolog.reshape(seqs * own, ch), coupling, entry, nonpadding.reshape(1, own),
-        w1, w2, wt, cg, wq, wo,
+        homolog.reshape(seqs * own, ch), coupling, entry.T, nonpadding.reshape(1, own),
+        w1.T, w2.T, wt, cg.T, wq, wo.T,
     )
     return pair_output, refreshed.reshape(seqs, own, ch)
 

time: 79.7 us -> 72.1 us (0.905)
  local copies, waits for them, and re-layouts: 11 us -> 4.79 us
  Pallas kernels: 67.7 us -> 66.5 us
    unnamed x12 -> x5, local copies, waits for them, and re-layouts: 11 us -> 4.79 us
    pallas_call x1, Pallas kernels: 67.7 us -> 66.5 us  [on_device(): pl.pallas_call(functools.partial(kernel, devices, seqs, own), out_shape=(...]
where the time goes in v3:
time: 72.1 us; the launch traced here: 71.9 us
  Pallas kernels  66.5 us (92%)
  local copies, waits for them, and re-layouts  4.79 us (7%)
    pallas_call x1, Pallas kernels, on_device(): pl.pallas_call(functools.partial(kernel, devices, seqs, own), out_shape=(...  66.5 us
    unnamed x5, local copies, waits for them, and re-layouts  4.79 us

profile of v3, /device:TPU:1, one launch (start us, length us, event | category | flops | bytes accessed | tf_op | source)
XLA Modules:
  0.0 71.9 jit_solution(17877627514021103119)
XLA Ops:
  0.6 2.0 %copy.12 = bf16[256,8,64]{2,1,0:T(8,128)(2,1)} copy(bf16[256,8,64]{0,2,1:T(8,128)(2,1)} %param.10) | data formatting | bytes 524288 | tf_op args[0]
  2.6 66.5 %shard_map.113 = (bf16[8,128,128]{2,1,0:T(8,128)(2,1)}, bf16[2048,64]{1,0:T(8,128)(2,1)}) custom-call(bf16[2048,64]{1,0:T(8,128)(2,1)} %bitcast.8, bf16[8,128,128]{2,1,0:T(8,128)(2,1)} %pair_ref.1, s32[8,256]{1,0:T(8,128)} %bitcast.11, s32[1,8]{1,0:T(1,128)} %bitcast.15, bf16[32,64]{1,0:T(8,128)(2,1)} %bitcast.12, bf16[32,64]{1,0:T(8,128)(2,1)} %bitcast.13, ...), custom_call_target="tpu_custom_call" | custom-call | tf_op jit(solution)/shard_map/pallas_call | solution.py:339
  69.1 0.0 copy-start
  69.2 2.1 %copy.13 = bf16[256,8,64]{0,2,1:T(8,128)(2,1)} copy(bf16[256,8,64]{2,1,0:T(8,128)(2,1)} %bitcast.9) | data formatting | bytes 524288
  71.2 0.0 copy-done
  71.2 0.7 copy.15
Async XLA Ops:
  69.1 2.1 %copy-start = (bf16[8,128,128]{2,1,0:T(8,128)(2,1)S(1)}, bf16[8,128,128]{2,1,0:T(8,128)(2,1)}, u32[]{:S(2)}) copy-start(bf16[8,128,128]{2,1,0:T(8,128)(2,1)} %get-tuple-element.10) | copy-start | bytes 786436
